TPU v7x, 32 devices: a whole 2x2x4 slice. The times are simulated.
32 devices in a mesh: span: 4 (over y, x), stream: 8 (over z, core).
Axes of the slice: x: 2, y: 2, z: 4, core: 2. Of those that a mesh axis runs over, the one named last changes fastest.
Arguments:
- state: float32 [6, 64, 16384], P(None, None, ('span', 'stream')), may hold values from -6 to 6
- stiffness: float32 [16384], P(('span', 'stream')), may hold values from 0.3 to 6
- crossing: int32 [2, 4096], P(None, ('span', 'stream')), may hold values from 0 to 511, as said below
- contact_send: int32 [2, 4, 32768], P(None, None, ('span', 'stream')), may hold values from 0 to 32767
- contact_recv: int32 [2, 4, 32768], P(None, None, ('span', 'stream')), may hold values from 0 to 32767
- contact_fill: int32 [2, 4, 256], P(None, None, ('span', 'stream')), may hold values from 0 to 128, as said below
Outputs:
- final_state: float32 [6, 64, 16384], P(None, None, ('span', 'stream'))
Inputs may be any that keep to these rules, and one draw needn't show every extreme that they name: `crossing`: each slab's 2 * 64 entries of one step are distinct and include slots 0 and 511. `contact_fill`: in each run of 8 blocks the live blocks come first; all full except the last live one; some runs have every block live.
All inputs are finite; a program needn't handle non-finite values.
Results may differ from a plain program's by a relative error of at most 0.0001.
Values sent between devices are 32-bit elements; how exact they have to be, the bound alone decides.
A program may use at most 128 MiB of HBM per device.

v0:
```python
import jax
import jax.numpy as jnp
from jax import lax
from jax.sharding import PartitionSpec as P

STEPS = 2


exact = lax.Precision.HIGHEST


def shifted(block, axis, distance):
    devices = range(lax.axis_size(axis))
    route = [((i - distance) % len(devices), i) for i in devices]
    return lax.ppermute(block, axis, route)


def thomas(coef, rhs):
    count = rhs.shape[1]
    first = 1.0 + coef
    cps = [-coef / first]
    ds = [rhs[:, 0] / first]
    for node in range(1, count):
        diag = 1.0 + coef if node == count - 1 else 1.0 + 2.0 * coef
        denom = diag + coef * cps[-1]
        cps.append(-coef / denom)
        ds.append((rhs[:, node] + coef * ds[-1]) / denom)
    outs = [ds[-1]]
    for node in range(count - 2, -1, -1):
        outs.append(ds[node] - cps[node] * outs[-1])
    return jnp.stack(outs[::-1], axis=1)


def slot_table(index, count):
    return (index[:, None] == jnp.arange(count, dtype=jnp.int32)[None, :]).astype(jnp.float32)


def node_table(index, count):
    return (jnp.arange(count, dtype=jnp.int32)[:, None] == index[None, :]).astype(jnp.float32)


def gather_nodes(positions, slot_hot, node_hot):
    picked = jnp.einsum("cnf,qf->cnq", positions, slot_hot, precision=exact)
    return jnp.sum(picked * node_hot[None], axis=1)


def pick_slots(fields_arr, hot):
    return jnp.einsum("cnf,kf->cnk", fields_arr, hot, precision=exact)


def pick_coef(coef, hot):
    return jnp.dot(hot, coef, precision=exact)


def migrate(leave_up, coef_up, leave_down, coef_down):
    from_above = shifted((leave_up, coef_up), "stream", 1)
    from_below = shifted((leave_down, coef_down), "stream", -1)
    return (from_above, from_below)


def per_device(state, stiffness, crossing, contact_send, contact_recv, contact_fill):
    fields, nodes, fdev = state.shape
    half = crossing.shape[1] // 2
    quota = contact_send.shape[2]
    groups = contact_send.shape[1]
    xcur = state
    coef = stiffness
    for step in range(STEPS):
        positions = xcur[:3]
        sidx = contact_send[step].reshape(-1)
        sent = gather_nodes(
            positions, slot_table(sidx % fdev, fdev), node_table(sidx // fdev, nodes)
        )
        sent = sent.reshape(3, groups, quota).transpose(1, 0, 2)
        sent_fill = contact_fill[step].astype(jnp.float32)
        got, got_fill = (
            lax.all_to_all(sent, "span", split_axis=0, concat_axis=0, tiled=True),
            lax.all_to_all(sent_fill, "span", split_axis=0, concat_axis=0, tiled=True),
        )
        ridx = contact_recv[step].reshape(-1)
        recv_slot = slot_table(ridx % fdev, fdev)
        recv_node = node_table(ridx // fdev, nodes)
        local = (
            gather_nodes(positions, recv_slot, recv_node)
            .reshape(3, groups, quota)
            .transpose(1, 0, 2)
        )
        delta = got - local
        radius = jnp.sum(delta * delta, axis=1, keepdims=True)
        lane = jnp.arange(128, dtype=jnp.float32)
        live = (lane[None, None, :] < got_fill[..., None]).reshape(groups, quota)
        force = jnp.where(live[:, None, :], 1.0 * delta / (1.0 + radius), 0.0)
        force_flat = force.transpose(1, 0, 2).reshape(3, -1)
        spread = force_flat[:, None, :] * recv_node[None]
        contact = jnp.einsum("cnq,qf->cnf", spread, recv_slot, precision=exact)
        rhs = jnp.concatenate([xcur[:3] + 0.5 * contact, xcur[3:]], axis=0)
        cross_hot = slot_table(crossing[step], fdev)
        solved = thomas(coef, rhs)
        leavers = pick_slots(solved, cross_hot)
        leaving_coef = pick_coef(coef, cross_hot)
        from_above, from_below = migrate(
            leavers[:, :, :half], leaving_coef[:half], leavers[:, :, half:], leaving_coef[half:]
        )
        keep = 1.0 - jnp.sum(cross_hot, axis=0)
        arrived = jnp.concatenate([from_above[0], from_below[0]], axis=2)
        arrived_coef = jnp.concatenate([from_above[1], from_below[1]], axis=0)
        xcur = solved * keep + jnp.einsum("cnk,kf->cnf", arrived, cross_hot, precision=exact)
        coef = coef * keep + jnp.dot(arrived_coef, cross_hot, precision=exact)
    return xcur


def solution(mesh):
    placed = (
        P(None, None, ("span", "stream")),
        P(("span", "stream")),
        P(None, ("span", "stream")),
        P(None, None, ("span", "stream")),
        P(None, None, ("span", "stream")),
        P(None, None, ("span", "stream")),
    )
    return jax.shard_map(
        per_device,
        mesh=mesh,
        in_specs=placed,
        out_specs=P(None, None, ("span", "stream")),
        check_vma=False,
    )
```

profile of v0, /device:TPU:0, one launch (start us, length us, event | category | flops | bytes accessed | tf_op | source)
XLA Modules:
  0.0 182.3 jit_solution(7224485375720400517)
XLA Ops:
  2.9 4.5 %collective-permute-start.3 = (f32[64]{0:T(128)}, f32[64]{0:T(128)}, u32[]{:S(2)}, u32[]{:S(2)}) collective-permute-start(f32[64]{0:T(128)} %get-tuple-element.669), channel_id=1, source_target_pairs={{1,0},{2,1},{3,2},{4,3},{5,4},{6,5},{7,6},{0,7},{9,8},{10,9},{11,1... | collective-permute-start | bytes 776 | tf_op jit(solution)/shard_map/ppermute | solution.py:15
  8.7 3.7 %all-to-all-start.2 = ((f32[4,1,8]{2,1,0:T(1,128)}), f32[4,1,8]{2,1,0:T(1,128)S(1)}, u32[]{:S(2)}, u32[]{:S(2)}) async-start(f32[4,1,8]{2,1,0:T(1,128)} %bitcast.101), calls=%async_computation.2 | async-start | bytes 4096 | tf_op jit(solution)/shard_map/all_to_all | solution.py:78
  26.0 1.3 negate_divide_fusion.102
  50.6 1.3 negate_divide_fusion.64
  57.5 1.3 convert_reduce_fusion
  58.9 6.2 %fusion.46 = f32[3,4096]{1,0:T(4,128)} fusion(f32[64,4096]{1,0:T(8,128)S(1)} %fusion.73, s32[4096]{0:T(1024)S(1)} %get-tuple-element.527, f32[6,64,512]{2,1,0:T(8,128)S(1)} %copy-done.2), kind=kOutput, calls=%fused_computation.284 | convolution fusion | flops 4835495936 | bytes 1507328 | tf_op jit(solution)/shard_map/cnf,qf->cnq/dot_general | solution.py:43
  65.1 5.5 %fusion.49 = f32[3,4096]{1,0:T(4,128)S(1)} fusion(f32[64,4096]{1,0:T(8,128)S(1)} %fusion.74, s32[4096]{0:T(1024)S(1)} %get-tuple-element.526, f32[6,64,512]{2,1,0:T(8,128)S(1)} %copy-done.2), kind=kOutput, calls=%fused_computation.285 | convolution fusion | flops 4835495936 | bytes 1507328 | tf_op jit(solution)/shard_map/cnf,qf->cnq/dot_general | solution.py:43
  70.7 4.2 %all-to-all-start = ((f32[4,1,8]{2,1,0:T(1,128)}), f32[4,1,8]{2,1,0:T(1,128)S(1)}, u32[]{:S(2)}, u32[]{:S(2)}) async-start(f32[4,1,8]{2,1,0:T(1,128)} %bitcast.2), calls=%async_computation | async-start | bytes 4096 | tf_op jit(solution)/shard_map/all_to_all | solution.py:78
  75.0 4.6 %all-to-all-done = f32[4,1,8]{2,1,0:T(1,128)S(1)} async-done(((f32[4,1,8]{2,1,0:T(1,128)}), f32[4,1,8]{2,1,0:T(1,128)S(1)}, u32[]{:S(2)}, u32[]{:S(2)}) %all-to-all-start) | async-done | bytes 160 | tf_op jit(solution)/shard_map/all_to_all | solution.py:78
  79.5 3.5 %all-to-all-start.1 = ((f32[4,3,1024]{2,1,0:T(4,128)}), f32[4,3,1024]{2,1,0:T(4,128)S(1)}, u32[]{:S(2)}, u32[]{:S(2)}) async-start(f32[4,3,1024]{2,1,0:T(4,128)} %bitcast.7), calls=%async_computation.1 | async-start | bytes 131072 | tf_op jit(solution)/shard_map/all_to_all | solution.py:77
  105.9 4.6 %fusion.68 = f32[3,64,512]{2,1,0:T(8,128)S(1)} fusion(s32[4096]{0:T(1024)} %copy-done.275, f32[3,4096]{1,0:T(4,128)S(1)} %bitcast.1692, f32[64,4096]{1,0:T(8,128)S(1)} %fusion.74, f32[6,64,512]{2,1,0:T(8,128)S(1)} %copy-done.2), kind=kOutput, calls=%fused_computation.292 | convolution fusion | flops 4834918400 | bytes 1900544 | tf_op jit(solution)/shard_map/cnq,qf->cnf/dot_general | solution.py:95
  112.0 1.3 broadcast_multiply_fusion.1
  121.3 1.3 subtract_bitcast_fusion.1
  127.4 1.5 collective-permute-start.1
  128.8 3.7 %collective-permute-done.1 = f32[6,64,64]{2,1,0:T(8,128)S(1)} collective-permute-done((f32[6,64,64]{2,1,0:T(8,128)S(1)}, f32[6,64,64]{2,1,0:T(8,128)S(1)}, u32[]{:S(2)}, u32[]{:S(2)}) %collective-permute-start.1) | collective-permute-done | bytes 98336 | tf_op jit(solution)/shard_map/ppermute | solution.py:15
  132.5 3.2 %collective-permute-done = f32[6,64,64]{2,1,0:T(8,128)S(1)} collective-permute-done((f32[6,64,64]{2,1,0:T(8,128)S(1)}, f32[6,64,64]{2,1,0:T(8,128)S(1)}, u32[]{:S(2)}, u32[]{:S(2)}) %collective-permute-start) | collective-permute-done | bytes 98336 | tf_op jit(solution)/shard_map/ppermute | solution.py:15
  136.3 6.2 %fusion.52 = f32[3,4096]{1,0:T(4,128)} fusion(f32[64,4096]{1,0:T(8,128)S(1)} %copy-done.1, f32[6,64,512]{2,1,0:T(8,128)S(1)} %convolution_add_fusion.1, s32[4096]{0:T(1024)S(1)} %copy-done.274), kind=kOutput, calls=%fused_computation.286 | convolution fusion | flops 4835495936 | bytes 1900544 | tf_op jit(solution)/shard_map/cnf,qf->cnq/dot_general | solution.py:43
  142.5 3.7 %all-to-all-start.3 = ((f32[4,3,1024]{2,1,0:T(4,128)}), f32[4,3,1024]{2,1,0:T(4,128)S(1)}, u32[]{:S(2)}, u32[]{:S(2)}) async-start(f32[4,3,1024]{2,1,0:T(4,128)} %bitcast.105), calls=%async_computation.3 | async-start | bytes 131072 | tf_op jit(solution)/shard_map/all_to_all | solution.py:77
  146.2 5.6 %fusion.55 = f32[3,4096]{1,0:T(4,128)S(1)} fusion(f32[64,4096]{1,0:T(8,128)S(1)} %fusion.76, f32[6,64,512]{2,1,0:T(8,128)S(1)} %convolution_add_fusion.1, s32[4096]{0:T(1024)S(1)} %copy-done.273), kind=kOutput, calls=%fused_computation.287 | convolution fusion | flops 4835495936 | bytes 1900544 | tf_op jit(solution)/shard_map/cnf,qf->cnq/dot_general | solution.py:43
  151.9 3.9 %slice_add_fusion = f32[3,64,512]{2,1,0:T(8,128)S(1)} fusion(f32[6,64,512]{2,1,0:T(8,128)S(1)} %convolution_add_fusion.1, s32[4096]{0:T(1024)S(1)} %copy-done.273, f32[3,4096]{1,0:T(4,128)S(1)} %bitcast.1691, f32[64,4096]{1,0:T(8,128)S(1)} %fusion.76), kind=kOutput, calls=%fused_computation.302 | convolution fusion | flops 4834918400 | bytes 1900544 | tf_op jit(solution)/shard_map/cnq,qf->cnf/dot_general | solution.py:95
  166.2 1.3 subtract_bitcast_fusion
  173.4 4.6 %collective-permute-done.5 = f32[6,64,64]{2,1,0:T(8,128)S(1)} collective-permute-done((f32[6,64,64]{2,1,0:T(8,128)S(1)}, f32[6,64,64]{2,1,0:T(8,128)S(1)}, u32[]{:S(2)}, u32[]{:S(2)}) %collective-permute-start.5) | collective-permute-done | bytes 98336 | tf_op jit(solution)/shard_map/ppermute | solution.py:15
  177.9 2.3 %collective-permute-done.4 = f32[6,64,64]{2,1,0:T(8,128)S(1)} collective-permute-done((f32[6,64,64]{2,1,0:T(8,128)S(1)}, f32[6,64,64]{2,1,0:T(8,128)S(1)}, u32[]{:S(2)}, u32[]{:S(2)}) %collective-permute-start.4) | collective-permute-done | bytes 98336 | tf_op jit(solution)/shard_map/ppermute | solution.py:15
  180.2 2.1 %convolution_add_fusion = f32[6,64,512]{2,1,0:T(8,128)} fusion(f32[6,64,512]{2,1,0:T(8,128)S(1)} %stack.267, f32[512]{0:T(512)S(1)} %broadcast_subtract_fusion, f32[6,64,64]{2,1,0:T(8,128)S(1)} %collective-permute-done.5, f32[6,64,64]{2,1,0:T(8,128)S(1)} %collective-permute-done.4, s32[128]{0:T(128)} %get-tuple-element.666), kind=kOutput, calls=%fused_computation.288 | convolution fusion | flops 302497792 | bytes 1772032 | tf_op jit(solution)/shard_map/cnk,kf->cnf/dot_general | solution.py:107
  (838 shorter events, 96.7 us)
Async XLA Ops:
  2.9 80.8 %collective-permute-start.3 = (f32[64]{0:T(128)}, f32[64]{0:T(128)}, u32[]{:S(2)}, u32[]{:S(2)}) collective-permute-start(f32[64]{0:T(128)} %get-tuple-element.669), channel_id=1, source_target_pairs={{1,0},{2,1},{3,2},{4,3},{5,4},{6,5},{7,6},{0,7},{9,8},{10,9},{11,1... | collective-permute-start | bytes 776 | tf_op jit(solution)/shard_map/ppermute | solution.py:15
  7.4 76.3 %collective-permute-start.2 = (f32[64]{0:T(128)}, f32[64]{0:T(128)}, u32[]{:S(2)}, u32[]{:S(2)}) collective-permute-start(f32[64]{0:T(128)} %get-tuple-element.668), channel_id=1, source_target_pairs={{7,0},{0,1},{1,2},{2,3},{3,4},{4,5},{5,6},{6,7},{15,8},{8,9},{9,10... | collective-permute-start | bytes 776 | tf_op jit(solution)/shard_map/ppermute | solution.py:15
  8.7 62.0 %all-to-all-start.2 = ((f32[4,1,8]{2,1,0:T(1,128)}), f32[4,1,8]{2,1,0:T(1,128)S(1)}, u32[]{:S(2)}, u32[]{:S(2)}) async-start(f32[4,1,8]{2,1,0:T(1,128)} %bitcast.101), calls=%async_computation.2 | async-start | bytes 4096 | tf_op jit(solution)/shard_map/all_to_all | solution.py:78
  14.4 40.4 %copy-start.23 = (f32[512]{0:T(512)}, f32[512]{0:T(512)S(1)}, u32[]{:S(2)}) copy-start(f32[512]{0:T(512)S(1)} %get-tuple-element.312) | copy-start | bytes 6148
  15.7 39.1 %copy-start.65 = (f32[512]{0:T(512)}, f32[512]{0:T(512)S(1)}, u32[]{:S(2)}) copy-start(f32[512]{0:T(512)S(1)} %get-tuple-element.571) | copy-start | bytes 6148
  17.0 37.8 %copy-start.67 = (f32[512]{0:T(512)}, f32[512]{0:T(512)S(1)}, u32[]{:S(2)}) copy-start(f32[512]{0:T(512)S(1)} %get-tuple-element.575) | copy-start | bytes 6148
  18.3 36.5 %copy-start.69 = (f32[512]{0:T(512)}, f32[512]{0:T(512)S(1)}, u32[]{:S(2)}) copy-start(f32[512]{0:T(512)S(1)} %get-tuple-element.318) | copy-start | bytes 6148
  19.5 35.2 %copy-start.71 = (f32[512]{0:T(512)}, f32[512]{0:T(512)S(1)}, u32[]{:S(2)}) copy-start(f32[512]{0:T(512)S(1)} %get-tuple-element.580) | copy-start | bytes 6148
  20.8 34.0 %copy-start.73 = (f32[512]{0:T(512)}, f32[512]{0:T(512)S(1)}, u32[]{:S(2)}) copy-start(f32[512]{0:T(512)S(1)} %get-tuple-element.322) | copy-start | bytes 6148
  22.1 32.7 %copy-start.75 = (f32[512]{0:T(512)}, f32[512]{0:T(512)S(1)}, u32[]{:S(2)}) copy-start(f32[512]{0:T(512)S(1)} %get-tuple-element.324) | copy-start | bytes 6148
  44.1 40.5 %copy-start.105 = (f32[512]{0:T(512)}, f32[512]{0:T(512)S(1)}, u32[]{:S(2)}) copy-start(f32[512]{0:T(512)S(1)} %get-tuple-element.361) | copy-start | bytes 6148
  45.4 39.2 %copy-start.107 = (f32[512]{0:T(512)}, f32[512]{0:T(512)S(1)}, u32[]{:S(2)}) copy-start(f32[512]{0:T(512)S(1)} %get-tuple-element.364) | copy-start | bytes 6148
  46.7 37.9 %copy-start.109 = (f32[512]{0:T(512)}, f32[512]{0:T(512)S(1)}, u32[]{:S(2)}) copy-start(f32[512]{0:T(512)S(1)} %get-tuple-element.367) | copy-start | bytes 6148
  48.1 36.6 %copy-start.111 = (f32[512]{0:T(512)}, f32[512]{0:T(512)S(1)}, u32[]{:S(2)}) copy-start(f32[512]{0:T(512)S(1)} %get-tuple-element.370) | copy-start | bytes 6148
  49.4 35.3 %copy-start.113 = (f32[512]{0:T(512)}, f32[512]{0:T(512)S(1)}, u32[]{:S(2)}) copy-start(f32[512]{0:T(512)S(1)} %get-tuple-element.373) | copy-start | bytes 6148
  50.6 34.1 %copy-start.115 = (f32[512]{0:T(512)}, f32[512]{0:T(512)S(1)}, u32[]{:S(2)}) copy-start(f32[512]{0:T(512)S(1)} %get-tuple-element.376) | copy-start | bytes 6148
  51.9 32.8 %copy-start.117 = (f32[512]{0:T(512)}, f32[512]{0:T(512)S(1)}, u32[]{:S(2)}) copy-start(f32[512]{0:T(512)S(1)} %get-tuple-element.379) | copy-start | bytes 6148
  70.7 8.9 %all-to-all-start = ((f32[4,1,8]{2,1,0:T(1,128)}), f32[4,1,8]{2,1,0:T(1,128)S(1)}, u32[]{:S(2)}, u32[]{:S(2)}) async-start(f32[4,1,8]{2,1,0:T(1,128)} %bitcast.2), calls=%async_computation | async-start | bytes 4096 | tf_op jit(solution)/shard_map/all_to_all | solution.py:78
  79.5 25.6 %all-to-all-start.1 = ((f32[4,3,1024]{2,1,0:T(4,128)}), f32[4,3,1024]{2,1,0:T(4,128)S(1)}, u32[]{:S(2)}, u32[]{:S(2)}) async-start(f32[4,3,1024]{2,1,0:T(4,128)} %bitcast.7), calls=%async_computation.1 | async-start | bytes 131072 | tf_op jit(solution)/shard_map/all_to_all | solution.py:77
  127.4 5.2 %collective-permute-start.1 = (f32[6,64,64]{2,1,0:T(8,128)S(1)}, f32[6,64,64]{2,1,0:T(8,128)S(1)}, u32[]{:S(2)}, u32[]{:S(2)}) collective-permute-start(f32[6,64,64]{2,1,0:T(8,128)S(1)} %get-tuple-element.514), channel_id=1, source_target_pairs={{1,0},{2,1},{3,2},{4,3},{5,4},{6,5},{7,6},{0,7},{9,8},{10,9},{11,1... | collective-permute-start | bytes 294920 | tf_op jit(solution)/shard_map/ppermute | solution.py:15
  128.8 6.9 %collective-permute-start = (f32[6,64,64]{2,1,0:T(8,128)S(1)}, f32[6,64,64]{2,1,0:T(8,128)S(1)}, u32[]{:S(2)}, u32[]{:S(2)}) collective-permute-start(f32[6,64,64]{2,1,0:T(8,128)S(1)} %get-tuple-element.513), channel_id=1, source_target_pairs={{7,0},{0,1},{1,2},{2,3},{3,4},{4,5},{5,6},{6,7},{15,8},{8,9},{9,10... | collective-permute-start | bytes 294920 | tf_op jit(solution)/shard_map/ppermute | solution.py:15
  142.5 9.3 %all-to-all-start.3 = ((f32[4,3,1024]{2,1,0:T(4,128)}), f32[4,3,1024]{2,1,0:T(4,128)S(1)}, u32[]{:S(2)}, u32[]{:S(2)}) async-start(f32[4,3,1024]{2,1,0:T(4,128)} %bitcast.105), calls=%async_computation.3 | async-start | bytes 131072 | tf_op jit(solution)/shard_map/all_to_all | solution.py:77
  172.8 5.2 %collective-permute-start.5 = (f32[6,64,64]{2,1,0:T(8,128)S(1)}, f32[6,64,64]{2,1,0:T(8,128)S(1)}, u32[]{:S(2)}, u32[]{:S(2)}) collective-permute-start(f32[6,64,64]{2,1,0:T(8,128)S(1)} %get-tuple-element.512), channel_id=1, source_target_pairs={{1,0},{2,1},{3,2},{4,3},{5,4},{6,5},{7,6},{0,7},{9,8},{10,9},{11,1... | collective-permute-start | bytes 294920 | tf_op jit(solution)/shard_map/ppermute | solution.py:15
  173.4 6.9 %collective-permute-start.4 = (f32[6,64,64]{2,1,0:T(8,128)S(1)}, f32[6,64,64]{2,1,0:T(8,128)S(1)}, u32[]{:S(2)}, u32[]{:S(2)}) collective-permute-start(f32[6,64,64]{2,1,0:T(8,128)S(1)} %get-tuple-element.511), channel_id=1, source_target_pairs={{7,0},{0,1},{1,2},{2,3},{3,4},{4,5},{5,6},{6,7},{15,8},{8,9},{9,10... | collective-permute-start | bytes 294920 | tf_op jit(solution)/shard_map/ppermute | solution.py:15
  (269 other events, 1202.5 us)
where the time goes:
time: 184 us; the launch traced here: 182 us
  other arithmetic  89.2 us (48%)
  matrix products  38.2 us (21%)
  starting transfers between devices  21.6 us (12%)
  waiting for transfers between devices  18.3 us (10%)
  local copies, waits for them, and re-layouts  10.7 us (6%)
  between operations  4.36 us (2%)
    div x52, other arithmetic, thomas(): cps.append(-coef / denom)  48.1 us
    dot_general x4, matrix products, gather_nodes(): picked = jnp.einsum('cnf,qf->cnq', positions, slot_hot, precision=exact)  23.5 us
    ppermute x6, waiting for transfers between devices, shifted(): return lax.ppermute(block, axis, route)  13.8 us
    another operation x20, other arithmetic, thomas(): return jnp.stack(outs[::-1], axis=1)  13.3 us
    add x11, other arithmetic, thomas(): denom = diag + coef * cps[-1]  10.8 us
    dot_general x2, matrix products, per_device(): contact = jnp.einsum('cnq,qf->cnf', spread, recv_slot, precision=exact)  8.48 us
    all_to_all x2, starting transfers between devices, per_device(): lax.all_to_all(sent_fill, 'span', split_axis=0, concat_axis=0, tiled=True)  7.92 us
    all_to_all x2, starting transfers between devices, per_device(): lax.all_to_all(sent, 'span', split_axis=0, concat_axis=0, tiled=True)  7.16 us
  transfers between devices with their start and end apart: 10, of which 5 were waited for; matrix products, arithmetic and copies ran while one was open for 47% of the time, Pallas kernels for 0%

commit v1 on v0

v1 whole, which is shorter than its diff:
```python
import functools
import math

import jax
import jax.numpy as jnp
import ml_dtypes
import numpy as np
from jax import lax
from jax.experimental import pallas as pl
from jax.experimental.pallas import tpu as pltpu
from jax.sharding import PartitionSpec as P

STEPS = 2
MESH = pl.DeviceIdType.MESH
F32 = jnp.float32
BF16 = jnp.bfloat16
LANES = 128
HALF_SLOTS = 256
SUB = 256


def cosine_tables(nodes):
    k = np.arange(nodes)[:, None]
    n = np.arange(nodes)[None, :]
    basis = np.sqrt(2.0 / nodes) * np.cos(np.pi * (n + 0.5) * k / nodes)
    basis[0] /= math.sqrt(2.0)

    def stacked(matrix):
        high = matrix.astype(ml_dtypes.bfloat16)
        low = (matrix - high.astype(np.float64)).astype(ml_dtypes.bfloat16)
        return np.concatenate([high, high, low], axis=1)

    lam = 2.0 - 2.0 * np.cos(np.pi * np.arange(nodes) / nodes)
    lam = np.repeat(lam[:, None], LANES, axis=1).astype(np.float32)
    return stacked(basis), stacked(basis.T), lam


def split(x):
    high = x.astype(BF16)
    return high, (x - high.astype(F32)).astype(BF16)


def split3(x):
    high, rest = x.astype(BF16), None
    rest = x - high.astype(F32)
    mid = rest.astype(BF16)
    return high, mid, (rest - mid.astype(F32)).astype(BF16)


def dot(a, b):
    return jnp.dot(a, b, preferred_element_type=F32)


def dot_nt(a, b):
    return lax.dot_general(a, b, (((1,), (1,)), ((), ())), preferred_element_type=F32)


def along_nodes(matrix, block):
    high, low = split(block)
    return dot(matrix, jnp.concatenate([high, low, high], axis=0))


def tall(row, rows):
    tile = jnp.broadcast_to(row, (16, row.shape[1])).astype(BF16)
    return jnp.concatenate([tile] * (rows // 16), axis=0)


def kernel(
    groups, n_stream,
    state, coef0, crossing, csend, crecv, cfill, fwd, inv, lam, iota,
    out,
    xh, parts, hot, local, acc, scale, coef_in, coef_out, sbuf, rbuf, mout, min_,
    c_send, c_recv, p_send, p_recv, m_send, m_recv,
):
    fields, nodes, fdev = state.shape
    quota = csend.shape[2]
    cross = crossing.shape[1]
    half = cross // 2
    npos = 3 * nodes
    rows = fields * nodes
    i = lax.axis_index("span")
    j = lax.axis_index("stream")
    down_dev = (i, lax.rem(j + 1, n_stream))
    up_dev = (i, lax.rem(j + n_stream - 1, n_stream))

    def mod(v):
        return lax.rem(v, groups)

    barrier = pltpu.get_barrier_semaphore()
    for dev in (down_dev, up_dev):
        pl.semaphore_signal(barrier, inc=1, device_id=dev, device_id_type=MESH)
    for k in range(1, groups):
        pl.semaphore_signal(
            barrier, inc=1, device_id=(mod(i + k), j), device_id_type=MESH
        )
    pl.semaphore_wait(barrier, groups + 1)

    lane = lax.broadcasted_iota(jnp.int32, (1, LANES), 1)
    node_iota = lax.broadcasted_iota(jnp.int32, (nodes, SUB), 0)

    def slot_hot(slot, q):
        pieces = []
        for part in range(fdev // HALF_SLOTS):
            rel = slot - part * HALF_SLOTS
            inside = (rel >= 0) & (rel < HALF_SLOTS)
            val = jnp.where(inside, rel, -1).astype(F32)
            wide = jnp.concatenate([iota[...]] * (q // LANES), axis=1)
            same = wide == tall(val, HALF_SLOTS)
            pieces.append(jnp.where(same, BF16(1), BF16(0)))
        return jnp.concatenate(pieces, axis=0)

    def gather(index, keep_at=None, sub=0):
        slot = lax.rem(index, fdev)
        node = lax.div(index, fdev)
        table = slot_hot(slot, SUB)
        if keep_at is not None:
            hot[keep_at, :, sub * SUB : (sub + 1) * SUB] = table
        picked = dot(parts[...], table)
        picked = picked[:npos] + picked[npos:]
        mask = node_iota == node
        return [
            jnp.sum(
                jnp.where(mask, picked[c * nodes : (c + 1) * nodes], 0.0),
                axis=0, keepdims=True,
            )
            for c in range(3)
        ]

    def set_parts(c, block):
        high, low = split(block)
        parts[c * nodes : (c + 1) * nodes, :] = high
        parts[npos + c * nodes : npos + (c + 1) * nodes, :] = low

    cross_hot = [slot_hot(crossing[s : s + 1, :], cross) for s in range(STEPS)]
    ones = jnp.ones((16, cross), BF16)
    keeps = [1.0 - dot_nt(ones, t)[:1] for t in cross_hot]

    coef = coef0[...]
    wide_coef = jnp.broadcast_to(coef, (16, fdev))
    leaving = sum(dot(p, cross_hot[0]) for p in split3(wide_coef))
    coef_out[...] = leaving[:8]
    coef_copies = [
        pltpu.make_async_remote_copy(
            src_ref=coef_out, dst_ref=coef_in.at[d],
            send_sem=c_send.at[d], recv_sem=c_recv.at[d],
            device_id=dev, device_id_type=MESH,
        )
        for d, dev in enumerate((down_dev, up_dev))
    ]
    for copy in coef_copies:
        copy.start()

    def set_scale(c):
        for b in range(fdev // LANES):
            at = slice(b * LANES, (b + 1) * LANES)
            scale[:, at] = 1.0 / (1.0 + lam[...] * c[:, at])

    def pair_copy(step, k):
        to = mod(i + 1 + k)
        return pltpu.make_async_remote_copy(
            src_ref=sbuf.at[step, to], dst_ref=rbuf.at[step, i],
            send_sem=p_send.at[step, to], recv_sem=p_recv.at[step, i],
            device_id=(to, j), device_id_type=MESH,
        )

    def pair_arrival(step, source):
        return pltpu.make_async_remote_copy(
            src_ref=sbuf.at[step, source], dst_ref=rbuf.at[step, source],
            send_sem=p_send.at[step, source], recv_sem=p_recv.at[step, source],
            device_id=(source, j), device_id_type=MESH,
        )

    for c in range(3):
        set_parts(c, state[c])

    for step in range(STEPS):

        def send_gather(g, buf):
            fill = cfill[step, pl.ds(g, 1), :]
            for sub in range(quota // SUB):
                at = slice(sub * SUB, (sub + 1) * SUB)
                got = gather(csend[step, pl.ds(g, 1), at])
                for c in range(3):
                    buf[c : c + 1, at] = got[c]
            for b in range(quota // LANES):
                live = lane < fill[:, b : b + 1]
                buf[3:4, b * LANES : (b + 1) * LANES] = jnp.where(live, 1.0, 0.0)

        @pl.loop(0, groups - 1)
        def _(k):
            to = mod(i + 1 + k)
            send_gather(to, sbuf.at[step, to])
            pair_copy(step, k).start()

        send_gather(i, rbuf.at[step, i])

        @pl.loop(0, groups)
        def _(g):
            for sub in range(quota // SUB):
                at = slice(sub * SUB, (sub + 1) * SUB)
                got = gather(crecv[step, pl.ds(g, 1), at], g, sub)
                for c in range(3):
                    local[g, c : c + 1, at] = got[c]

        if step == 0:
            set_scale(coef)
            for c in range(fields):
                xh[c * nodes : (c + 1) * nodes, :] = along_nodes(fwd[...], state[c])
        else:
            for copy in coef_copies:
                copy.wait()
            arrived = jnp.where(
                lax.broadcasted_iota(jnp.int32, (8, cross), 1) < half,
                coef_in[0], coef_in[1],
            )
            arrived = jnp.concatenate([arrived, arrived], axis=0)
            moved = sum(dot_nt(p, cross_hot[0]) for p in split3(arrived))
            set_scale(coef * keeps[0] + moved[:1])

        acc[...] = jnp.zeros_like(acc)

        def scatter(g):
            delta = rbuf[step, g, 0:3] - local[g, 0:3]
            radius = jnp.sum(delta * delta, axis=0, keepdims=True)
            live = rbuf[step, g, 3:4] > 0.5
            force = jnp.where(live, 0.5 * delta / (1.0 + radius), 0.0)
            node = lax.div(crecv[step, pl.ds(g, 1), :], fdev).astype(F32)
            wide = jnp.concatenate([iota[:nodes]] * (quota // LANES), axis=1)
            node_hot = jnp.where(wide == tall(node, nodes), BF16(1), BF16(0))
            high, low = split(force)
            spread = [
                node_hot * tall(p[c : c + 1].astype(F32), nodes)
                for p in (high, low)
                for c in range(3)
            ]
            acc[...] += dot_nt(jnp.concatenate(spread, axis=0), hot[g])

        scatter(i)

        @pl.loop(0, groups - 1)
        def _(k):
            source = mod(i + groups - 1 - k)
            pair_arrival(step, source).wait_recv()
            scatter(source)

        for c in range(fields):
            at = slice(c * nodes, (c + 1) * nodes)
            block = xh[at, :]
            if c < 3:
                low_at = slice(npos + c * nodes, npos + (c + 1) * nodes)
                block += along_nodes(fwd[...], acc[at, :] + acc[low_at, :])
            xh[at, :] = block * scale[...]

        table = cross_hot[step]
        high, low = split(xh[...])
        picked = dot(high, table) + dot(low, table)
        top, bottom = picked[: rows // 2], picked[rows // 2 :]
        first = lax.broadcasted_iota(jnp.int32, (rows // 2, cross), 1) < half
        mout[step, 0] = jnp.where(first, top, pltpu.roll(bottom, half, 1))
        mout[step, 1] = jnp.where(first, pltpu.roll(top, half, 1), bottom)
        copies = [
            pltpu.make_async_remote_copy(
                src_ref=mout.at[step, d], dst_ref=min_.at[step, d],
                send_sem=m_send.at[step, d], recv_sem=m_recv.at[step, d],
                device_id=dev, device_id_type=MESH,
            )
            for d, dev in enumerate((down_dev, up_dev))
        ]
        for copy in copies:
            copy.start()
        for copy in copies:
            copy.wait()
        above, below = min_[step, 0], min_[step, 1]
        came = jnp.concatenate(
            [
                jnp.where(first, above, pltpu.roll(below, half, 1)),
                jnp.where(first, pltpu.roll(above, half, 1), below),
            ],
            axis=0,
        )
        high, low = split(came)
        xh[...] = xh[...] * keeps[step] + dot_nt(high, table) + dot_nt(low, table)

        if step < STEPS - 1:
            for c in range(3):
                block = xh[c * nodes : (c + 1) * nodes, :]
                set_parts(c, along_nodes(inv[...], block))
        else:
            for c in range(fields):
                block = xh[c * nodes : (c + 1) * nodes, :]
                out[c] = along_nodes(inv[...], block)

    for step in range(STEPS):

        @pl.loop(0, groups - 1)
        def _(k):
            pair_copy(step, k).wait_send()


def per_device(groups, n_stream, state, stiffness, crossing, csend, crecv, cfill):
    fields, nodes, fdev = state.shape
    quota = csend.shape[2]
    cross = crossing.shape[1]
    rows = fields * nodes
    fwd, inv, lam = cosine_tables(nodes)
    iota = np.repeat(np.arange(HALF_SLOTS)[:, None], LANES, axis=1)
    iota = iota.astype(ml_dtypes.bfloat16)
    vmem = pl.BlockSpec(memory_space=pltpu.VMEM)
    return pl.pallas_call(
        functools.partial(kernel, groups, n_stream),
        out_shape=jax.ShapeDtypeStruct(state.shape, F32),
        in_specs=[vmem] * 10,
        out_specs=vmem,
        scratch_shapes=[
            pltpu.VMEM((rows, fdev), F32),
            pltpu.VMEM((6 * nodes, fdev), BF16),
            pltpu.VMEM((groups, fdev, quota), BF16),
            pltpu.VMEM((groups, 4, quota), F32),
            pltpu.VMEM((6 * nodes, fdev), F32),
            pltpu.VMEM((nodes, fdev), F32),
            pltpu.VMEM((2, 8, cross), F32),
            pltpu.VMEM((8, cross), F32),
            pltpu.VMEM((STEPS, groups, 4, quota), F32),
            pltpu.VMEM((STEPS, groups, 4, quota), F32),
            pltpu.VMEM((STEPS, 2, rows // 2, cross), F32),
            pltpu.VMEM((STEPS, 2, rows // 2, cross), F32),
            pltpu.SemaphoreType.DMA((2,)),
            pltpu.SemaphoreType.DMA((2,)),
            pltpu.SemaphoreType.DMA((STEPS, groups)),
            pltpu.SemaphoreType.DMA((STEPS, groups)),
            pltpu.SemaphoreType.DMA((STEPS, 2)),
            pltpu.SemaphoreType.DMA((STEPS, 2)),
        ],
        compiler_params=pltpu.CompilerParams(
            collective_id=0, has_side_effects=True, vmem_limit_bytes=48 * 2**20
        ),
    )(
        state, stiffness.reshape(1, fdev), crossing, csend, crecv, cfill,
        jnp.asarray(fwd), jnp.asarray(inv), jnp.asarray(lam), jnp.asarray(iota),
    )


def solution(mesh):
    cells = ("span", "stream")
    placed = (
        P(None, None, cells),
        P(cells),
        P(None, cells),
        P(None, None, cells),
        P(None, None, cells),
        P(None, None, cells),
    )
    return jax.shard_map(
        functools.partial(per_device, mesh.shape["span"], mesh.shape["stream"]),
        mesh=mesh,
        in_specs=placed,
        out_specs=P(None, None, cells),
        check_vma=False,
    )
```

time: 184 us -> 41.2 us (0.22)
  other arithmetic: 89.2 us -> 0 us
  matrix products: 38.2 us -> 0 us
  Pallas kernels: 0 us -> 31.9 us
  starting transfers between devices: 21.6 us -> 0 us
  waiting for transfers between devices: 18.3 us -> 0 us
  between operations: 4.36 us -> 0.02 us
  local copies, waits for them, and re-layouts: 10.7 us -> 8.69 us
    div x55 -> x0, other arithmetic: 49.4 us -> none  [the longest x52 48.1 us: thomas(): cps.append(-coef / denom)]
    dot_general x12 -> x0, matrix products: 38.2 us -> none  [the longest x4 23.5 us: gather_nodes(): picked = jnp.einsum('cnf,qf->cnq', positions, slot_hot, precision=exact)]
    pallas_call x0 -> x1, Pallas kernels: none -> 31.9 us  [per_device(): pl.pallas_call(functools.partial(kernel, groups, n_stream), out_shape=jax...]
    all_to_all x4 -> x0, starting transfers between devices: 15.1 us -> none  [the longest x2 7.92 us: per_device(): lax.all_to_all(sent_fill, 'span', split_axis=0, concat_axis=0, tiled=True)]
    ppermute x6 -> x0, waiting for transfers between devices: 13.8 us -> none  [shifted(): return lax.ppermute(block, axis, route)]
    another operation x20 -> x0, other arithmetic: 13.3 us -> none  [thomas(): return jnp.stack(outs[::-1], axis=1)]
    add x13 -> x0, other arithmetic: 10.8 us -> none  [the longest x11 10.8 us: thomas(): denom = diag + coef * cps[-1]]
    ppermute x6 -> x0, starting transfers between devices: 6.53 us -> none  [shifted(): return lax.ppermute(block, axis, route)]
  transfers between devices with their start and end apart: 10 -> 0, of which waited for: 5 -> 0; matrix products, arithmetic and copies ran while one was open for 47% -> 0% of each run, Pallas kernels for 0% -> 0%
where the time goes in v1:
time: 41.2 us; the launch traced here: 40.6 us
  Pallas kernels  31.9 us (77%)
  local copies, waits for them, and re-layouts  8.69 us (21%)
    pallas_call x1, Pallas kernels, per_device(): pl.pallas_call(functools.partial(kernel, groups, n_stream), out_shape=jax...  31.9 us
    unnamed x21, local copies, waits for them, and re-layouts  8.69 us

profile of v1, /device:TPU:0, one launch (start us, length us, event | category | flops | bytes accessed | tf_op | source)
XLA Modules:
  0.0 40.6 jit_solution(1131371461549599543)
XLA Ops:
  0.0 0.0 copy-start.9
  0.0 0.7 %copy-done.9 = s32[2,128]{1,0:T(2,128)S(1)} copy-done((s32[2,128]{1,0:T(2,128)S(1)}, s32[2,128]{1,0:T(2,128)}, u32[]{:S(2)}) %copy-start.9) | copy-done | bytes 1048
  0.7 0.0 copy-start
  0.7 1.1 %copy-done = f32[6,64,512]{2,1,0:T(8,128)S(1)} copy-done((f32[6,64,512]{2,1,0:T(8,128)S(1)}, f32[6,64,512]{2,1,0:T(8,128)}, u32[]{:S(2)}) %copy-start) | copy-done | bytes 786456
  1.8 0.0 copy-start.1
  1.8 0.8 %copy-done.1 = bf16[256,128]{1,0:T(8,128)(2,1)S(1)} copy-done((bf16[256,128]{1,0:T(8,128)(2,1)S(1)}, bf16[256,128]{1,0:T(8,128)(2,1)}, u32[]{:S(2)}) %copy-start.1) | copy-done | bytes 65560
  2.7 0.0 copy-start.2
  2.7 0.8 %copy-done.2 = s32[2,4,1024]{2,1,0:T(4,128)S(1)} copy-done((s32[2,4,1024]{2,1,0:T(4,128)S(1)}, s32[2,4,1024]{2,1,0:T(4,128)}, u32[]{:S(2)}) %copy-start.2) | copy-done | bytes 32792
  3.4 0.0 copy-start.3
  3.4 0.8 %copy-done.3 = s32[2,4,1024]{2,1,0:T(4,128)S(1)} copy-done((s32[2,4,1024]{2,1,0:T(4,128)S(1)}, s32[2,4,1024]{2,1,0:T(4,128)}, u32[]{:S(2)}) %copy-start.3) | copy-done | bytes 32792
  4.2 0.0 copy-start.4
  4.2 0.8 %copy-done.4 = f32[64,128]{1,0:T(8,128)S(1)} copy-done((f32[64,128]{1,0:T(8,128)S(1)}, f32[64,128]{1,0:T(8,128)}, u32[]{:S(2)}) %copy-start.4) | copy-done | bytes 32792
  4.9 0.0 copy-start.5
  4.9 0.8 %copy-done.5 = bf16[64,192]{1,0:T(8,128)(2,1)S(1)} copy-done((bf16[64,192]{1,0:T(8,128)(2,1)S(1)}, bf16[64,192]{1,0:T(8,128)(2,1)}, u32[]{:S(2)}) %copy-start.5) | copy-done | bytes 24600
  5.7 0.0 copy-start.6
  5.7 0.8 %copy-done.6 = bf16[64,192]{1,0:T(8,128)(2,1)S(1)} copy-done((bf16[64,192]{1,0:T(8,128)(2,1)S(1)}, bf16[64,192]{1,0:T(8,128)(2,1)}, u32[]{:S(2)}) %copy-start.6) | copy-done | bytes 24600
  6.4 0.0 copy-start.7
  6.4 0.7 %copy-done.7 = s32[2,4,8]{2,1,0:T(4,128)S(1)} copy-done((s32[2,4,8]{2,1,0:T(4,128)S(1)}, s32[2,4,8]{2,1,0:T(4,128)}, u32[]{:S(2)}) %copy-start.7) | copy-done | bytes 280
  7.1 0.0 copy-start.8
  7.1 0.7 %copy-done.8 = f32[512]{0:T(512)S(1)} copy-done((f32[512]{0:T(512)S(1)}, f32[512]{0:T(512)}, u32[]{:S(2)}) %copy-start.8) | copy-done | bytes 2072
  7.8 31.9 %shard_map.100 = f32[6,64,512]{2,1,0:T(8,128)S(1)} custom-call(f32[6,64,512]{2,1,0:T(8,128)S(1)} %copy-done, f32[1,512]{1,0:T(1,128)S(1)} %bitcast.1, s32[2,128]{1,0:T(2,128)S(1)} %copy-done.9, s32[2,4,1024]{2,1,0:T(4,128)S(1)} %copy-done.2, s32[2,4,1024]{2,1,0:T(4,128)S(1)} %copy-done.3, s32[2,4,8]{2,1,0:T(4,128)S(1)} %copy-done.7, ...), custom_call_target="tpu_custom_call" | custom-call | tf_op jit(solution)/shard_map/pallas_call | solution.py:309
  39.7 0.9 %copy.12 = f32[6,64,512]{2,1,0:T(8,128)} copy(f32[6,64,512]{2,1,0:T(8,128)S(1)} %shard_map.100) | data formatting | bytes 1572864
Async XLA Ops:
  0.0 0.7 %copy-start.9 = (s32[2,128]{1,0:T(2,128)S(1)}, s32[2,128]{1,0:T(2,128)}, u32[]{:S(2)}) copy-start(s32[2,128]{1,0:T(2,128)} %crossing.1) | copy-start | bytes 3076
  0.7 1.1 %copy-start = (f32[6,64,512]{2,1,0:T(8,128)S(1)}, f32[6,64,512]{2,1,0:T(8,128)}, u32[]{:S(2)}) copy-start(f32[6,64,512]{2,1,0:T(8,128)} %state.1) | copy-start | bytes 2359300
  1.8 0.8 %copy-start.1 = (bf16[256,128]{1,0:T(8,128)(2,1)S(1)}, bf16[256,128]{1,0:T(8,128)(2,1)}, u32[]{:S(2)}) copy-start(bf16[256,128]{1,0:T(8,128)(2,1)} %constant.11.clone.iota) | copy-start | bytes 196612
  2.7 0.8 %copy-start.2 = (s32[2,4,1024]{2,1,0:T(4,128)S(1)}, s32[2,4,1024]{2,1,0:T(4,128)}, u32[]{:S(2)}) copy-start(s32[2,4,1024]{2,1,0:T(4,128)} %csend.1) | copy-start | bytes 98308
  3.4 0.8 %copy-start.3 = (s32[2,4,1024]{2,1,0:T(4,128)S(1)}, s32[2,4,1024]{2,1,0:T(4,128)}, u32[]{:S(2)}) copy-start(s32[2,4,1024]{2,1,0:T(4,128)} %crecv.1) | copy-start | bytes 98308
  4.2 0.8 %copy-start.4 = (f32[64,128]{1,0:T(8,128)S(1)}, f32[64,128]{1,0:T(8,128)}, u32[]{:S(2)}) copy-start(f32[64,128]{1,0:T(8,128)} %constant.10.clone.lam) | copy-start | bytes 98308
  4.9 0.8 %copy-start.5 = (bf16[64,192]{1,0:T(8,128)(2,1)S(1)}, bf16[64,192]{1,0:T(8,128)(2,1)}, u32[]{:S(2)}) copy-start(bf16[64,192]{1,0:T(8,128)(2,1)} %constant.9.clone.inv) | copy-start | bytes 73732
  5.7 0.8 %copy-start.6 = (bf16[64,192]{1,0:T(8,128)(2,1)S(1)}, bf16[64,192]{1,0:T(8,128)(2,1)}, u32[]{:S(2)}) copy-start(bf16[64,192]{1,0:T(8,128)(2,1)} %constant.8.clone.fwd) | copy-start | bytes 73732
  6.4 0.7 %copy-start.7 = (s32[2,4,8]{2,1,0:T(4,128)S(1)}, s32[2,4,8]{2,1,0:T(4,128)}, u32[]{:S(2)}) copy-start(s32[2,4,8]{2,1,0:T(4,128)} %cfill.1) | copy-start | bytes 772
  7.1 0.7 %copy-start.8 = (f32[512]{0:T(512)S(1)}, f32[512]{0:T(512)}, u32[]{:S(2)}) copy-start(f32[512]{0:T(512)} %param.11) | copy-start | bytes 6148
